TPU v7x, 128 devices: a whole 4x4x4 slice. The times are simulated.
128 devices in a mesh: row: 4 (over y), col: 16 (over x, z_hi, core), depth: 2 (over z_lo).
Axes of the slice: x: 4, y: 4, z: 4 (z_hi: 2, z_lo: 2; z = z_hi * 2 + z_lo), core: 2. Of those that a mesh axis runs over, the one named last changes fastest.
Arguments:
- values: bfloat16 [800, 80, 128, 128], P(('row', 'depth'), 'col'), may hold values from -2 to 2
- pattern: int32 [800, 80], P(('row', 'depth'), 'col'), may hold values from 0 to 49, as said below
- branch_flag: int32 [40], replicated, may hold values from 0 to 1, as said below
Outputs:
- purified: bfloat16 [40, 80, 128, 128], P(('row', 'depth'), 'col')
Inputs may be any that keep to these rules, and one draw needn't show every extreme that they name: `pattern`: block columns fall into classes with 5 members in every column panel; block (i, j) is nonzero exactly when i and j are in the same class, and the 5 slots of a block row in panel c list, in no particular order, the distinct panel-local indices of the members of its class in that panel. `branch_flag`: exactly half of the entries, rounded down, are 1; the rest are 0.
All inputs are finite; a program needn't handle non-finite values.
Results may differ from a plain program's by a relative error of at most 0.001.
Values may be sent and summed in bfloat16 or wider, within the bound.
A program may use at most 128 MiB of HBM per device.

v0:
```python
import jax
import jax.numpy as jnp
from jax import lax
from jax.sharding import PartitionSpec as P

SLAB_DEV = 5


def broadcast(block, axis, holder):
    block = jnp.where(lax.axis_index(axis) == holder, block, jnp.zeros_like(block))
    return lax.psum(block, axis)


def body(values, pattern, branch_flag):
    groups = lax.axis_size(("row", "depth"))
    shard_index = lax.axis_index(("row", "depth"))
    panels = lax.axis_size("col")
    rows_here = values.shape[0]
    slot_count = values.shape[1]
    block_size = values.shape[2]
    total_rows = rows_here * groups
    panel_cols = total_rows // panels
    stride = rows_here // SLAB_DEV
    panel_count = max(1, rows_here // panel_cols)
    first_panel = shard_index * rows_here // panel_cols
    mine_vals = values[::stride]
    mine_cols = pattern[::stride]
    slab_vals, slab_cols = (
        lax.all_gather(mine_vals, ("row", "depth"), axis=0, tiled=True),
        lax.all_gather(mine_cols, ("row", "depth"), axis=0, tiled=True),
    )
    piece_vals = []
    piece_cols = []
    for offset in range(panel_count):
        root_panel = first_panel + offset
        got_vals, got_cols = (
            broadcast(slab_vals, "col", root_panel),
            broadcast(slab_cols, "col", root_panel),
        )
        piece_vals.append(got_vals)
        piece_cols.append(got_cols + root_panel * panel_cols)
    left_vals = jnp.concatenate(piece_vals, 1)
    left_cols = jnp.concatenate(piece_cols, 1)
    slab_total = left_vals.shape[0]
    left_slots = left_vals.shape[1]
    local_rows = left_cols - shard_index * rows_here
    inside = (local_rows >= 0) & (local_rows < rows_here)
    local_rows = jnp.clip(local_rows, 0, rows_here - 1).astype(jnp.int32)
    left_vals = jnp.where(inside[:, :, None, None], left_vals, jnp.zeros((), left_vals.dtype))
    right_cols = pattern[local_rows]
    match = right_cols[:, :, None, :] == slab_cols[:, None, :, None]
    present = jnp.any(match, axis=3)
    slot_iota = lax.broadcasted_iota(jnp.int32, match.shape, 3)
    chosen = jnp.sum(jnp.where(match, slot_iota, 0), axis=3)
    group_rows = slab_total // groups

    def group_product(items):
        block_vals, row_index, slot_index, live = items
        picked = values[row_index[:, :, None], slot_index]
        picked = jnp.where(live[:, :, :, None, None], picked, jnp.zeros((), picked.dtype))
        return jnp.einsum(
            "ilab,ilmbc->imac", block_vals, picked, preferred_element_type=jnp.float32
        )

    partial_terms = lax.map(
        group_product,
        (
            left_vals.reshape(groups, group_rows, left_slots, block_size, block_size),
            local_rows.reshape(groups, group_rows, left_slots),
            chosen.reshape(groups, group_rows, left_slots, slot_count),
            present.reshape(groups, group_rows, left_slots, slot_count),
        ),
    )
    partial_terms = partial_terms.reshape(slab_total, slot_count, block_size, block_size)
    summed = lax.psum_scatter(partial_terms, ("row", "depth"), scatter_dimension=0, tiled=True)
    own_count = mine_vals.shape[0]
    own_flags = lax.dynamic_slice_in_dim(branch_flag, shard_index * own_count, own_count)
    own = mine_vals.astype(jnp.float32)
    result = jnp.where(own_flags[:, None, None, None] == 1, summed, 2.0 * own - summed)
    return result.astype(jnp.bfloat16)


def solution(mesh):
    in_specs = (P(("row", "depth"), "col", None, None), P(("row", "depth"), "col"), P())
    out_specs = P(("row", "depth"), "col", None, None)
    return jax.shard_map(body, mesh=mesh, in_specs=in_specs, out_specs=out_specs, check_vma=False)
```

profile of v0, /device:TPU:1, one launch (start us, length us, event | category | flops | bytes accessed | tf_op | source)
XLA Modules:
  0.0 1057.2 jit_solution(11381887055578751937)
XLA Ops:
  6.5 2.1 slice.7
  8.8 137.5 %all-gather.3.cloned.1.call-done = bf16[40,5,128,128]{3,2,1,0:T(8,128)(2,1)} async-done(((bf16[5,5,128,128]{3,2,1,0:T(8,128)(2,1)}), bf16[40,5,128,128]{3,2,1,0:T(8,128)(2,1)}) %all-gather.3.cloned.1.call-update) | async-done | bytes 6553616 | tf_op jit(solution)/shard_map/all_gather | solution.py:29
  146.2 8.4 broadcast_select_fusion.1
  155.4 30.0 %all-gather = s32[8,5,5]{2,1,0:T(8,128)S(1)} all-gather(s32[1,5,5]{2,1,0:T(8,128)S(1)} %bitcast.59), channel_id=1, replica_groups=mesh['row'=4,'col'=16,'depth'=2] {'row','depth'}, dimensions={0}, use_global_device_ids=true | all-gather | bytes 900 | tf_op jit(solution)/shard_map/all_gather | solution.py:30
  185.5 15.9 %all-reduce = (s32[40,5]{0,1:T(8,128)S(1)}, s32[40,5]{0,1:T(8,128)S(1)}) all-reduce(s32[40,5]{0,1:T(8,128)S(1)} %get-tuple-element.92, s32[40,5]{0,1:T(8,128)S(1)} %get-tuple-element.91), channel_id=1, replica_groups=mesh['row'=4,'col'=16,'depth'=2] {'col'}, use_global_device_ids=true, to_apply=%region_1.2 | all-reduce | flops 400 | bytes 3200 | tf_op jit(solution)/shard_map/psum | solution.py:11
  204.9 248.1 %all-reduce.4.cloned.1.call-done = (bf16[8,5,5,128,128]{4,3,2,1,0:T(8,128)(2,1)}, bf16[8,5,5,128,128]{4,3,2,1,0:T(8,128)(2,1)}) async-done(((bf16[8,5,5,128,128]{4,3,2,1,0:T(8,128)(2,1)}, bf16[8,5,5,128,128]{4,3,2,1,0:T(8,128)(2,1)}), (bf16[8,5,5,128,128]{4,3,2,1,0:T(8,128)(2,1)}, bf16[8,5,5,128,128]{4,3,2,1,0:T(8,128)(2,1)})) %all-reduce.4.cloned.1.call-update) | async-done | bytes 13107216 | tf_op jit(solution)/shard_map/psum | solution.py:11
  453.0 10.1 maximum_select_fusion
  463.1 327.5 %while.10 = (s32[]{:T(128)}, f32[8,5,5,128,128]{4,3,2,1,0:T(8,128)}, pred[8,5,10,5]{2,3,1,0:T(8,128)(4,1)S(1)}, s32[8,5,10]{2,1,0:T(8,128)S(1)}, s32[8,5,10,5]{3...) while((s32[]{:T(128)}, ...), condition=%wide.region_7.8_spmd, body=%wide.region_6.7_spmd.sunk | while | flops 1052673728 | bytes 50798872 | solution.py:65
  464.1 17.9 %gather_fusion = bf16[250,128,128]{2,1,0:T(8,128)(2,1)} fusion(bf16[100,5,128,128]{3,2,1,0:T(8,128)(2,1)} %get-tuple-element.159, s32[250]{0:T(256)S(1)} %reshape.163), kind=kCustom, calls=%fused_computation.clone.1 | custom fusion | bytes 16386000 | tf_op jit(solution)/shard_map/while/body/eval_jaxpr/gather | solution.py:59
  482.1 12.8 %copy.65 = bf16[5,10,5,128,128]{3,4,1,2,0:T(8,128)(2,1)} copy(bf16[5,10,5,128,128]{4,3,2,1,0:T(8,128)(2,1)} %bitcast.52) | data formatting | bytes 16384000 | tf_op jit(solution)/shard_map/while/body/eval_jaxpr/gather | solution.py:59
  494.9 6.1 fusion.31
  501.0 1.8 copy.66
  502.8 1.3 constant_dynamic-update-slice_fusion.2
  505.0 17.9 %gather_fusion = bf16[250,128,128]{2,1,0:T(8,128)(2,1)} fusion(bf16[100,5,128,128]{3,2,1,0:T(8,128)(2,1)} %get-tuple-element.159, s32[250]{0:T(256)S(1)} %reshape.163), kind=kCustom, calls=%fused_computation.clone.1 | custom fusion | bytes 16386000 | tf_op jit(solution)/shard_map/while/body/eval_jaxpr/gather | solution.py:59
  523.0 12.8 %copy.65 = bf16[5,10,5,128,128]{3,4,1,2,0:T(8,128)(2,1)} copy(bf16[5,10,5,128,128]{4,3,2,1,0:T(8,128)(2,1)} %bitcast.52) | data formatting | bytes 16384000 | tf_op jit(solution)/shard_map/while/body/eval_jaxpr/gather | solution.py:59
  535.8 6.1 fusion.31
  541.9 1.8 copy.66
  543.7 1.3 constant_dynamic-update-slice_fusion.2
  546.0 17.9 %gather_fusion = bf16[250,128,128]{2,1,0:T(8,128)(2,1)} fusion(bf16[100,5,128,128]{3,2,1,0:T(8,128)(2,1)} %get-tuple-element.159, s32[250]{0:T(256)S(1)} %reshape.163), kind=kCustom, calls=%fused_computation.clone.1 | custom fusion | bytes 16386000 | tf_op jit(solution)/shard_map/while/body/eval_jaxpr/gather | solution.py:59
  563.9 12.8 %copy.65 = bf16[5,10,5,128,128]{3,4,1,2,0:T(8,128)(2,1)} copy(bf16[5,10,5,128,128]{4,3,2,1,0:T(8,128)(2,1)} %bitcast.52) | data formatting | bytes 16384000 | tf_op jit(solution)/shard_map/while/body/eval_jaxpr/gather | solution.py:59
  576.8 6.1 fusion.31
  582.9 1.8 copy.66
  584.6 1.3 constant_dynamic-update-slice_fusion.2
  586.9 17.9 %gather_fusion = bf16[250,128,128]{2,1,0:T(8,128)(2,1)} fusion(bf16[100,5,128,128]{3,2,1,0:T(8,128)(2,1)} %get-tuple-element.159, s32[250]{0:T(256)S(1)} %reshape.163), kind=kCustom, calls=%fused_computation.clone.1 | custom fusion | bytes 16386000 | tf_op jit(solution)/shard_map/while/body/eval_jaxpr/gather | solution.py:59
  604.8 12.8 %copy.65 = bf16[5,10,5,128,128]{3,4,1,2,0:T(8,128)(2,1)} copy(bf16[5,10,5,128,128]{4,3,2,1,0:T(8,128)(2,1)} %bitcast.52) | data formatting | bytes 16384000 | tf_op jit(solution)/shard_map/while/body/eval_jaxpr/gather | solution.py:59
  617.7 6.1 fusion.31
  623.8 1.8 copy.66
  625.6 1.3 constant_dynamic-update-slice_fusion.2
  627.8 17.9 %gather_fusion = bf16[250,128,128]{2,1,0:T(8,128)(2,1)} fusion(bf16[100,5,128,128]{3,2,1,0:T(8,128)(2,1)} %get-tuple-element.159, s32[250]{0:T(256)S(1)} %reshape.163), kind=kCustom, calls=%fused_computation.clone.1 | custom fusion | bytes 16386000 | tf_op jit(solution)/shard_map/while/body/eval_jaxpr/gather | solution.py:59
  645.8 12.8 %copy.65 = bf16[5,10,5,128,128]{3,4,1,2,0:T(8,128)(2,1)} copy(bf16[5,10,5,128,128]{4,3,2,1,0:T(8,128)(2,1)} %bitcast.52) | data formatting | bytes 16384000 | tf_op jit(solution)/shard_map/while/body/eval_jaxpr/gather | solution.py:59
  658.6 6.1 fusion.31
  664.7 1.8 copy.66
  668.7 17.9 %gather_fusion = bf16[250,128,128]{2,1,0:T(8,128)(2,1)} fusion(bf16[100,5,128,128]{3,2,1,0:T(8,128)(2,1)} %get-tuple-element.159, s32[250]{0:T(256)S(1)} %reshape.163), kind=kCustom, calls=%fused_computation.clone.1 | custom fusion | bytes 16386000 | tf_op jit(solution)/shard_map/while/body/eval_jaxpr/gather | solution.py:59
  686.7 12.8 %copy.65 = bf16[5,10,5,128,128]{3,4,1,2,0:T(8,128)(2,1)} copy(bf16[5,10,5,128,128]{4,3,2,1,0:T(8,128)(2,1)} %bitcast.52) | data formatting | bytes 16384000 | tf_op jit(solution)/shard_map/while/body/eval_jaxpr/gather | solution.py:59
  699.5 6.1 fusion.31
  705.6 1.8 copy.66
  707.4 1.3 constant_dynamic-update-slice_fusion.2
  709.7 17.9 %gather_fusion = bf16[250,128,128]{2,1,0:T(8,128)(2,1)} fusion(bf16[100,5,128,128]{3,2,1,0:T(8,128)(2,1)} %get-tuple-element.159, s32[250]{0:T(256)S(1)} %reshape.163), kind=kCustom, calls=%fused_computation.clone.1 | custom fusion | bytes 16386000 | tf_op jit(solution)/shard_map/while/body/eval_jaxpr/gather | solution.py:59
  727.6 12.8 %copy.65 = bf16[5,10,5,128,128]{3,4,1,2,0:T(8,128)(2,1)} copy(bf16[5,10,5,128,128]{4,3,2,1,0:T(8,128)(2,1)} %bitcast.52) | data formatting | bytes 16384000 | tf_op jit(solution)/shard_map/while/body/eval_jaxpr/gather | solution.py:59
  740.5 6.1 fusion.31
  746.6 1.8 copy.66
  750.6 17.9 %gather_fusion = bf16[250,128,128]{2,1,0:T(8,128)(2,1)} fusion(bf16[100,5,128,128]{3,2,1,0:T(8,128)(2,1)} %get-tuple-element.159, s32[250]{0:T(256)S(1)} %reshape.163), kind=kCustom, calls=%fused_computation.clone.1 | custom fusion | bytes 16386000 | tf_op jit(solution)/shard_map/while/body/eval_jaxpr/gather | solution.py:59
  768.5 12.8 %copy.65 = bf16[5,10,5,128,128]{3,4,1,2,0:T(8,128)(2,1)} copy(bf16[5,10,5,128,128]{4,3,2,1,0:T(8,128)(2,1)} %bitcast.52) | data formatting | bytes 16384000 | tf_op jit(solution)/shard_map/while/body/eval_jaxpr/gather | solution.py:59
  781.4 6.1 fusion.31
  787.5 1.8 copy.66
  789.3 1.4 constant_dynamic-update-slice_fusion.2
  791.4 256.4 %reduce-scatter.2.cloned.1.call-done = f32[5,5,128,128]{3,2,1,0:T(8,128)} async-done(((f32[40,5,128,128]{3,2,1,0:T(8,128)}), f32[5,5,128,128]{3,2,1,0:T(8,128)}) %reduce-scatter.2.cloned.1.call-update) | async-done | bytes 1638416 | tf_op jit(solution)/shard_map/reduce_scatter | solution.py:75
  1047.8 2.9 fusion.18
  (70 shorter events, 15.6 us)
Async XLA Ops:
  6.5 139.7 %all-gather.3.cloned.1.call-start = ((), (), s32[]{:S(2)}) async-start(), calls=%async_computation.1 | async-start | bytes 7372800 | tf_op jit(solution)/shard_map/all_gather | solution.py:29
  8.7 444.4 %all-reduce.4.cloned.1.call-start = ((), (), s32[]{:S(2)}) async-start(), calls=%async_computation.3 | async-start | bytes 26214400 | tf_op jit(solution)/shard_map/psum | solution.py:11
  154.6 0.7 copy-start
  154.6 893.1 %reduce-scatter.2.cloned.1.call-start = ((), (), s32[]{:S(2)}) async-start(), calls=%async_computation.2 | async-start | bytes 14745600 | tf_op jit(solution)/shard_map/reduce_scatter | solution.py:75
  790.6 0.7 copy-start.1
Sparse Core Ops, SparseCore 0:
  9.0 137.1 all-gather.2
  154.8 298.2 all-reduce.3
  790.8 256.9 reduce-scatter.1
where the time goes:
time: 1060 us
  waiting for transfers between devices  642 us (61%)
  local copies, waits for them, and re-layouts  278 us (26%)
  matrix products  48.7 us (5%)
  blocking collectives  45.9 us (4%)
  other arithmetic  28.6 us (3%)
  between operations  13.2 us (1%)
    reduce_scatter x1, waiting for transfers between devices, body(): lax.psum_scatter(partial_terms, ('row', 'depth'), scatter_dimension=0, ti...  256 us
    psum x1, waiting for transfers between devices, broadcast(): return lax.psum(block, axis)  248 us
    gather x16, local copies, waits for them, and re-layouts, group_product(): picked = values[row_index[:, :, None], slot_index]  246 us
    all_gather x1, waiting for transfers between devices, body(): lax.all_gather(mine_vals, ('row', 'depth'), axis=0, tiled=True)  137 us
    dot_general x8, matrix products, group_product(): jnp.einsum('ilab,ilmbc->imac', block_vals, picked, preferred_element_type...  48.7 us
    all_gather x1, blocking collectives, body(): lax.all_gather(mine_cols, ('row', 'depth'), axis=0, tiled=True)  30 us
    dynamic_update_slice x16, local copies, waits for them, and re-layouts, body(): lax.map(group_product, (left_vals.reshape(groups, group_rows, left_slots,...  24.6 us
  transfers between devices with their start and end apart: 3, of which 3 were waited for; matrix products, arithmetic and copies ran while one was open for 0% of the time, Pallas kernels for 0%

commit v1 on v0

v1 whole, which is shorter than its diff:
```python
import functools

import jax
import jax.numpy as jnp
from jax import lax
from jax.experimental import pallas as pl
from jax.experimental.pallas import tpu as pltpu
from jax.sharding import PartitionSpec as P

W = 5
B = 128
WL = 5
R = WL * B
PR = R + 16
MESH = pl.DeviceIdType.MESH
F32 = jnp.float32
BF16 = jnp.bfloat16
TOP = 32512.0
STEPS = 128.0


def encode(dst, p):
    amax = jnp.max(jnp.abs(p), axis=0, keepdims=True)
    e = jnp.ceil(jnp.log2(jnp.maximum(amax, 1e-30)) * STEPS)
    q = jnp.round(p * (jnp.exp2(e * (-1.0 / STEPS)) * TOP)).astype(jnp.int32).astype(jnp.int16)
    for m in range(WL):
        dst[m * B : (m + 1) * B, :] = q[:, m * B : (m + 1) * B]
    e = e.astype(jnp.int32)
    rows = [e[:, m * B : (m + 1) * B] for m in range(WL)] + [jnp.zeros((16 - WL, B), jnp.int32)]
    dst[R:PR, :] = jnp.concatenate(rows, axis=0).astype(jnp.int16)


def decode(src):
    e = src[R:PR, :].astype(jnp.int32).astype(F32)
    scale = jnp.exp2(e * (1.0 / STEPS)) * (1.0 / TOP)
    parts = []
    for m in range(WL):
        q = src[m * B : (m + 1) * B, :].astype(jnp.int32).astype(F32)
        parts.append(q * scale[m : m + 1, :])
    return jnp.concatenate(parts, axis=1)


def kernel(
    flag_ref, vals, pat, out,
    rbuf, sbuf, lbuf, psend, precv, ctile, crecv, ktile, krecv, acc, idxv, idxs,
    ld_sem, r_sem, t_send, l_send, l_recv, p_send, p_recv, c_send, c_recv, k_send, k_recv, i_sem,
):
    y = lax.axis_index("row")
    zl = lax.axis_index("depth")
    col = lax.axis_index("col")
    x = col // 4
    zh = (col // 2) % 2
    core = col % 2
    g = y * 2 + zl

    def dev(dx, dy, dzh, dzl, dcore):
        return {"row": dy, "col": dx * 4 + dzh * 2 + dcore, "depth": dzl}

    xp, xm = (x + 1) % 4, (x + 3) % 4
    sib = dev(x, y, zh, zl, 1 - core)
    zx = dev(x, y, 1 - zh, zl, core)
    xpd, xmd = dev(xp, y, zh, zl, core), dev(xm, y, zh, zl, core)
    t_to = dev((x + y) % 4, x, zl, zh, core)
    t_from = dev(y, (x + 4 - y) % 4, zl, zh, core)
    away = jnp.logical_or(jnp.logical_or((x + y) % 4 != x, x != y), zl != zh)

    def source(cx, czh):
        return ((cx + 4 - y) % 4) * 2 + czh

    def group_dev(t):
        return dev(x, t // 2, zh, t % 2, core)

    def own_copy(w):
        return pltpu.make_async_copy(vals.at[pl.ds(20 * w * WL, WL)], sbuf.at[w], ld_sem.at[w])

    r_copy = pltpu.make_async_copy(vals, rbuf, r_sem)

    barrier = pltpu.get_barrier_semaphore()

    def greet(d):
        pl.semaphore_signal(barrier, inc=1, device_id=d, device_id_type=MESH)

    for d in (sib, zx, xpd, xmd):
        greet(d)
    for o in range(1, 8):
        greet(group_dev((g + o) % 8))

    @pl.when(away)
    def _():
        greet(t_to)
        greet(t_from)

    lane = lax.broadcasted_iota(jnp.int32, (1, B), 1)
    mine = jnp.logical_and(lane >= g * 16, lane < g * 16 + 16)
    ctile[...] = jnp.zeros((W, 8, B), jnp.int32)
    ktile[0] = jnp.zeros((8, B), jnp.int32)
    for w in range(W):
        krow = jnp.zeros((1, B), jnp.int32)
        for s in range(WL):
            v = jnp.broadcast_to(pat[20 * w : 20 * w + 1, s : s + 1], (1, B))
            ctile[w, s : s + 1, :] = jnp.where(mine, v, 0)
            krow = jnp.where(lane == g * 16 + core * WL + s, v + core * 50, krow)
        ktile[0, w : w + 1, :] = krow

    @pl.when(away)
    def _():
        pl.semaphore_wait(barrier, 13)

    @pl.when(jnp.logical_not(away))
    def _():
        pl.semaphore_wait(barrier, 11)

    def remote(src, dst, ssem, rsem, d):
        return pltpu.make_async_remote_copy(
            src_ref=src, dst_ref=dst, send_sem=ssem, recv_sem=rsem, device_id=d, device_id_type=MESH
        )

    def t_copy(w):
        return remote(
            vals.at[pl.ds(20 * w * WL, WL)], lbuf.at[w, g, core], t_send.at[w], l_recv.at[w, g, core], t_to
        )

    def t_start(w):
        @pl.when(away)
        def _():
            t_copy(w).start()

        @pl.when(jnp.logical_not(away))
        def _():
            pltpu.make_async_copy(
                vals.at[pl.ds(20 * w * WL, WL)], lbuf.at[w, g, core], l_recv.at[w, g, core]
            ).start()

    def k_copy(src, k, d):
        return remote(src, krecv.at[k], k_send.at[k], k_recv.at[k], d)

    def k_start():
        @pl.when(away)
        def _():
            k_copy(ktile.at[0], 0, t_to).start()

        @pl.when(jnp.logical_not(away))
        def _():
            pltpu.make_async_copy(ktile.at[0], krecv.at[0], k_recv.at[0]).start()

    def k_got(k):
        k_copy(ktile.at[0], k, sib).wait_recv()

    def c_copy(o):
        return remote(ctile, crecv.at[g], c_send.at[o - 1], c_recv.at[g], group_dev((g + o) % 8))

    def piece_copy(w, gs, d, k):
        slot = lbuf.at[w, gs, core]
        return remote(slot, slot, l_send.at[w, k], l_recv.at[w, gs, core], d)

    def got(w, gs, p):
        slot = lbuf.at[w, gs, p]
        remote(slot, slot, l_send.at[w, 0], l_recv.at[w, gs, p], sib).wait_recv()

    own = source(x, zh)
    ownz = source(x, 1 - zh)
    left = source(xm, zh)
    leftz = source(xm, 1 - zh)
    right = source(xp, zh)
    rightz = source(xp, 1 - zh)
    far0 = source((x + 2) % 4, 0)
    far1 = source((x + 2) % 4, 1)
    sends = (
        (own, zx), (own, xpd), (own, xmd), (own, sib),
        (ownz, xpd), (ownz, xmd), (ownz, sib),
        (source(xm, 0), xpd), (source(xp, 1), xmd),
        (left, sib), (leftz, sib), (right, sib), (rightz, sib),
        (far0, sib), (far1, sib),
    )

    def send(w, *numbers):
        for k in numbers:
            piece_copy(w, sends[k][0], sends[k][1], k).start()

    def relay_a(w):
        got(w, own, core)
        send(w, 0, 1, 2, 3)

    def relay_b(w):
        got(w, ownz, core)
        send(w, 4, 5, 6)

    def relay_c(w):
        for gs in (left, right, leftz, rightz):
            got(w, gs, core)
        send(w, 7, 8, 9, 10, 11, 12)

    def relay_d(w):
        got(w, far0, core)
        got(w, far1, core)
        send(w, 13, 14)

    def relay_e(w):
        for gs in range(8):
            got(w, gs, 1 - core)

    def make_index():
        total = ktile[2] + krecv[3] + krecv[4] + krecv[5]
        rows = lax.broadcasted_iota(jnp.int32, (100, B), 0)
        slots = [jnp.broadcast_to(pat[:, s : s + 1], (100, B)) for s in range(WL)]
        for w in range(W):
            kv = total[w : w + 1, :]
            here = rows == kv
            cols = ctile[w]
            for o in range(1, 8):
                cols = cols + crecv[(g + o) % 8, w]
            idx = jnp.broadcast_to(kv * WL, (8, B))
            for s in range(1, WL):
                right = jnp.sum(jnp.where(here, slots[s], 0), axis=0, keepdims=True)
                idx = idx + jnp.where(right == cols, s, 0)
            idxv[w] = idx
        copy = pltpu.make_async_copy(idxv, idxs, i_sem)
        copy.start()
        copy.wait()

    def product(w, gs):
        lc = jnp.concatenate(
            [lbuf[w, gs, p, s] for p in range(2) for s in range(WL)], axis=1
        )

        def block(m, l):
            return rbuf[idxs[w, m, gs * 16 + l]]

        rc = jnp.concatenate(
            [jnp.concatenate([block(m, l) for m in range(WL)], axis=1) for l in range(2 * WL)], axis=0
        )
        return jnp.dot(lc, rc, preferred_element_type=F32)

    def p_copy(w, k, d):
        return remote(psend.at[w, k], precv.at[w, k], p_send.at[w, k], p_recv.at[w, k], d)

    def y_dev(t):
        return dev(x, (y + 1 + 2 * t) % 4, zh, zl, core)

    zl_dev = dev(x, y, zh, 1 - zl, core)

    def pair(step):
        def body(t, carry):
            step(t)
            return carry

        lax.fori_loop(0, 2, body, 0)

    def far_rows(w):
        def step(t):
            encode(psend.at[w, t], product(w, ((y + 2) % 4) * 2 + t))
            p_copy(w, t, y_dev(t)).start()

        pair(step)

    def near_rows(w):
        def step(t):
            encode(psend.at[w, 2 + t], product(w, ((y + 1 + 2 * t) % 4) * 2 + 1 - t))
            p_copy(w, 2 + t, y_dev(t)).start()

        pair(step)

    def own_rows(w):
        def step(t):
            acc[w % 2, t] = product(w, y * 2 + t)

        pair(step)

    def joined_rows(w):
        def step(t):
            p = product(w, ((y + 1 + 2 * t) % 4) * 2 + t)
            p_copy(w, t, y_dev(t)).wait_recv()
            encode(psend.at[w, 4 + t], p + decode(precv.at[w, t]))
            p_copy(w, 4 + t, y_dev(t)).start()

        pair(step)

    def plane_sum(w, tz):
        a, b = 4 - 2 * tz, 3 + 2 * tz
        p_copy(w, b, zl_dev).wait_recv()
        p_copy(w, a, zl_dev).wait_recv()
        return acc[w % 2, tz] + decode(precv.at[w, a]) + decode(precv.at[w, b])

    def cross(w):
        encode(psend.at[w, 6], plane_sum(w, 1 - zl))
        p_copy(w, 6, zl_dev).start()

    def finish(w):
        own_copy(w).wait()
        s = plane_sum(w, zl)
        p_copy(w, 6, zl_dev).wait_recv()
        s = s + decode(precv.at[w, 6])
        plain = flag_ref[g * WL + w] == 1
        c_s = jnp.where(plain, 1.0, -1.0)
        c_o = jnp.where(plain, 0.0, 2.0)
        for m in range(WL):
            o = sbuf[w, m].astype(F32)
            out[w, m] = (
                c_s * s[:, m * B : (m + 1) * B] + c_o * o
            ).astype(BF16)

    t_start(0)
    k_start()
    t_start(1)
    for o in range(1, 8):
        c_copy(o).start()
    r_copy.start()
    k_got(0)
    k_copy(krecv.at[0], 1, sib).start()
    relay_a(0)
    t_start(2)
    k_got(1)
    ktile[1] = krecv[0] + krecv[1]
    k_copy(ktile.at[1], 2, zx).start()
    relay_b(0)
    t_start(3)
    relay_a(1)
    k_got(2)
    ktile[2] = ktile[1] + krecv[2]
    k_copy(ktile.at[2], 3, xpd).start()
    k_copy(ktile.at[2], 4, xmd).start()
    relay_b(1)
    relay_c(0)
    t_start(4)
    k_got(3)
    k_got(4)
    k_copy(krecv.at[3], 5, xpd).start()
    for w in range(W):
        own_copy(w).start()
    for o in range(1, 8):
        remote(
            ctile, crecv.at[(g + o) % 8], c_send.at[o - 1], c_recv.at[(g + o) % 8], sib
        ).wait_recv()
    relay_d(0)
    k_got(5)
    make_index()
    r_copy.wait()

    def wave(w, carry):
        def guard(cond, f, v):
            @pl.when(cond)
            def _():
                f(v)

        def first(v):
            relay_e(v)
            far_rows(v)

        guard(w < W, first, w)
        guard(w < W - 2, relay_a, w + 2)
        guard(w < W, near_rows, w)
        guard(w < W - 1, relay_c, w + 1)
        guard(w < W - 2, relay_b, w + 2)
        guard(w < W, own_rows, w)
        guard(w < W, joined_rows, w)
        guard(w < W - 1, relay_d, w + 1)
        return carry

    def wave_tail(w, carry):
        @pl.when(w > 0)
        def _():
            cross(w - 1)

        wave_body(w)

        @pl.when(w > 0)
        def _():
            finish(w - 1)

        return carry

    def wave_body(w):
        @pl.when(w < W)
        def _():
            wave(w, 0)

    lax.fori_loop(0, W + 1, wave_tail, 0)

    def drain(w, carry):
        @pl.when(away)
        def _():
            t_copy(w).wait_send()

        for k in range(15):
            piece_copy(w, sends[k][0], sends[k][1], k).wait_send()
        for k in range(7):
            p_copy(w, k, zl_dev).wait_send()
        return carry

    lax.fori_loop(0, W, drain, 0)
    for o in range(1, 8):
        c_copy(o).wait_send()

    @pl.when(away)
    def _():
        k_copy(ktile.at[0], 0, t_to).wait_send()

    for k in range(1, 6):
        k_copy(ktile.at[0], k, sib).wait_send()


def body(values, pattern, branch_flag):
    vmem = pl.BlockSpec(memory_space=pltpu.VMEM)
    dma = pltpu.SemaphoreType.DMA
    return pl.pallas_call(
        kernel,
        out_shape=jax.ShapeDtypeStruct((W, WL, B, B), BF16),
        in_specs=[pl.BlockSpec(memory_space=pltpu.SMEM), pl.BlockSpec(memory_space=pl.ANY), vmem],
        out_specs=vmem,
        scratch_shapes=[
            pltpu.VMEM((500, B, B), BF16),
            pltpu.VMEM((W, WL, B, B), BF16),
            pltpu.VMEM((W, 8, 2, WL, B, B), BF16),
            pltpu.VMEM((W, 7, PR, B), jnp.int16),
            pltpu.VMEM((W, 7, PR, B), jnp.int16),
            pltpu.VMEM((W, 8, B), jnp.int32),
            pltpu.VMEM((8, W, 8, B), jnp.int32),
            pltpu.VMEM((3, 8, B), jnp.int32),
            pltpu.VMEM((6, 8, B), jnp.int32),
            pltpu.VMEM((2, 2, B, R), F32),
            pltpu.VMEM((W, 8, B), jnp.int32),
            pltpu.SMEM((W, 8, B), jnp.int32),
            dma((W,)), dma, dma((W,)), dma((W, 15)), dma((W, 8, 2)), dma((W, 7)), dma((W, 7)),
            dma((7,)), dma((8,)), dma((6,)), dma((6,)), dma,
        ],
        compiler_params=pltpu.CompilerParams(
            collective_id=0, has_side_effects=True, vmem_limit_bytes=58 * 2**20
        ),
        cost_estimate=pl.CostEstimate(flops=8_400_000_000, bytes_accessed=20_000_000, transcendentals=0),
    )(branch_flag, values.reshape(500, B, B), pattern)


def solution(mesh):
    in_specs = (P(("row", "depth"), "col", None, None), P(("row", "depth"), "col"), P())
    out_specs = P(("row", "depth"), "col", None, None)
    return jax.shard_map(body, mesh=mesh, in_specs=in_specs, out_specs=out_specs, check_vma=False)
```

time: 1060 us -> 126 us (0.12)
  waiting for transfers between devices: 642 us -> 0 us
  local copies, waits for them, and re-layouts: 278 us -> 3.53 us
  Pallas kernels: 0 us -> 120 us
  matrix products: 48.7 us -> 0 us
  blocking collectives: 45.9 us -> 0 us
  other arithmetic: 28.6 us -> 0 us
  between operations: 13.2 us -> 0.01 us
    reduce_scatter x1 -> x0, waiting for transfers between devices: 256 us -> none  [body(): lax.psum_scatter(partial_terms, ('row', 'depth'), scatter_dimension=0, ti...]
    psum x1 -> x0, waiting for transfers between devices: 248 us -> none  [broadcast(): return lax.psum(block, axis)]
    gather x20 -> x0, local copies, waits for them, and re-layouts: 248 us -> none  [the longest x16 246 us: group_product(): picked = values[row_index[:, :, None], slot_index]]
    all_gather x1 -> x0, waiting for transfers between devices: 137 us -> none  [body(): lax.all_gather(mine_vals, ('row', 'depth'), axis=0, tiled=True)]
    pallas_call x0 -> x1, Pallas kernels: none -> 120 us  [body(): pl.pallas_call(kernel, out_shape=jax.ShapeDtypeStruct((W, WL, B, B), BF16...]
    dot_general x8 -> x0, matrix products: 48.7 us -> none  [group_product(): jnp.einsum('ilab,ilmbc->imac', block_vals, picked, preferred_element_type...]
    all_gather x1 -> x0, blocking collectives: 30 us -> none  [body(): lax.all_gather(mine_cols, ('row', 'depth'), axis=0, tiled=True)]
    dynamic_update_slice x16 -> x0, local copies, waits for them, and re-layouts: 24.6 us -> none  [body(): lax.map(group_product, (left_vals.reshape(groups, group_rows, left_slots,...]
  transfers between devices with their start and end apart: 3 -> 0, of which waited for: 3 -> 0; matrix products, arithmetic and copies ran while one was open for 0% -> 0% of each run, Pallas kernels for 0% -> 0%
where the time goes in v1:
time: 126 us; the launch traced here: 124 us
  Pallas kernels  120 us (95%)
  local copies, waits for them, and re-layouts  3.53 us (3%)
    pallas_call x1, Pallas kernels, body(): pl.pallas_call(kernel, out_shape=jax.ShapeDtypeStruct((W, WL, B, B), BF16...  120 us
    unnamed x2, local copies, waits for them, and re-layouts  3.53 us

profile of v1, /device:TPU:1, one launch (start us, length us, event | category | flops | bytes accessed | tf_op | source)
XLA Modules:
  0.0 123.6 jit_solution(10862766066221479456)
XLA Ops:
  0.0 1.4 %copy.4.pat = s32[100,5]{1,0:T(8,128)} copy(s32[100,5]{0,1:T(8,128)} %param.4) | data formatting | bytes 4000 | tf_op args[1]
  1.4 120.0 %shard_map.37 = bf16[5,5,128,128]{3,2,1,0:T(8,128)(2,1)} custom-call(s32[40]{0:T(128)} %flag_ref.1, bf16[500,128,128]{2,1,0:T(8,128)(2,1)} %bitcast.1, s32[100,5]{1,0:T(8,128)} %copy.4.pat), custom_call_target="tpu_custom_call" | custom-call | flops 8400000000 | bytes 20000000 | tf_op jit(solution)/shard_map/pallas_call | solution.py:405
  121.4 2.1 %copy.6 = bf16[5,5,128,128]{3,2,1,0:T(8,128)(2,1)} copy(bf16[5,5,128,128]{3,2,1,0:T(8,128)(2,1)} %shard_map.37) | data formatting | bytes 1638400

commit v2 on v1

--- a/solution.py
+++ b/solution.py
@@ -53,6 +53,11 @@
     core = col % 2
     g = y * 2 + zl
 
+    def spread(a, b, p):
+        a, b = a * (1 + 2 * p) % 4, b * (1 + 2 * p) % 4
+        a1, a0, b1, b0 = a // 2, a % 2, b // 2, b % 2
+        return (((a0 + a1 + b0) % 2) * 2 + (a1 + b0 + b1) % 2) * (1 + 2 * p) % 4
+
     def dev(dx, dy, dzh, dzl, dcore):
         return {"row": dy, "col": dx * 4 + dzh * 2 + dcore, "depth": dzl}
 
@@ -60,12 +65,13 @@
     sib = dev(x, y, zh, zl, 1 - core)
     zx = dev(x, y, 1 - zh, zl, core)
     xpd, xmd = dev(xp, y, zh, zl, core), dev(xm, y, zh, zl, core)
-    t_to = dev((x + y) % 4, x, zl, zh, core)
-    t_from = dev(y, (x + 4 - y) % 4, zl, zh, core)
-    away = jnp.logical_or(jnp.logical_or((x + y) % 4 != x, x != y), zl != zh)
-
-    def source(cx, czh):
-        return ((cx + 4 - y) % 4) * 2 + czh
+    to_x = spread(x, y, core)
+    t_to = dev(to_x, x, zl, zh, core)
+    t_from = dev(y, to_x, zl, zh, core)
+    away = jnp.logical_or(x != y, zl != zh)
+
+    def place(gs, p):
+        return spread(y, gs // 2, p) * 2 + gs % 2
 
     def group_dev(t):
         return dev(x, t // 2, zh, t % 2, core)
@@ -91,15 +97,16 @@
         greet(t_from)
 
     lane = lax.broadcasted_iota(jnp.int32, (1, B), 1)
-    mine = jnp.logical_and(lane >= g * 16, lane < g * 16 + 16)
-    ctile[...] = jnp.zeros((W, 8, B), jnp.int32)
+    ctile[...] = jnp.zeros((8, B), jnp.int32)
     ktile[0] = jnp.zeros((8, B), jnp.int32)
     for w in range(W):
+        crow = jnp.zeros((1, B), jnp.int32)
         krow = jnp.zeros((1, B), jnp.int32)
         for s in range(WL):
             v = jnp.broadcast_to(pat[20 * w : 20 * w + 1, s : s + 1], (1, B))
-            ctile[w, s : s + 1, :] = jnp.where(mine, v, 0)
+            crow = jnp.where(lane == s, v, crow)
             krow = jnp.where(lane == g * 16 + core * WL + s, v + core * 50, krow)
+        ctile[w : w + 1, :] = crow
         ktile[0, w : w + 1, :] = krow
 
     @pl.when(away)
@@ -117,7 +124,11 @@
 
     def t_copy(w):
         return remote(
-            vals.at[pl.ds(20 * w * WL, WL)], lbuf.at[w, g, core], t_send.at[w], l_recv.at[w, g, core], t_to
+            vals.at[pl.ds(20 * w * WL, WL)],
+            lbuf.at[w, to_x * 2 + zl, core],
+            t_send.at[w],
+            l_recv.at[w, to_x * 2 + zl, core],
+            t_to,
         )
 
     def t_start(w):
@@ -127,8 +138,9 @@
 
         @pl.when(jnp.logical_not(away))
         def _():
+            slot = x * 2 + zl
             pltpu.make_async_copy(
-                vals.at[pl.ds(20 * w * WL, WL)], lbuf.at[w, g, core], l_recv.at[w, g, core]
+                vals.at[pl.ds(20 * w * WL, WL)], lbuf.at[w, slot, core], l_recv.at[w, slot, core]
             ).start()
 
     def k_copy(src, k, d):
@@ -149,82 +161,85 @@
     def c_copy(o):
         return remote(ctile, crecv.at[g], c_send.at[o - 1], c_recv.at[g], group_dev((g + o) % 8))
 
-    def piece_copy(w, gs, d, k):
-        slot = lbuf.at[w, gs, core]
-        return remote(slot, slot, l_send.at[w, k], l_recv.at[w, gs, core], d)
-
-    def got(w, gs, p):
-        slot = lbuf.at[w, gs, p]
-        remote(slot, slot, l_send.at[w, 0], l_recv.at[w, gs, p], sib).wait_recv()
-
-    own = source(x, zh)
-    ownz = source(x, 1 - zh)
-    left = source(xm, zh)
-    leftz = source(xm, 1 - zh)
-    right = source(xp, zh)
-    rightz = source(xp, 1 - zh)
-    far0 = source((x + 2) % 4, 0)
-    far1 = source((x + 2) % 4, 1)
+    def got(w, q, p):
+        slot = lbuf.at[w, q, p]
+        remote(slot, slot, l_send.at[w, 0], l_recv.at[w, q, p], sib).wait_recv()
+
+    on_x, back_x = (x + 1 + 2 * core) % 4, (x + 3 + 2 * core) % 4
+    on, back = dev(on_x, y, zh, zl, core), dev(back_x, y, zh, zl, core)
+    q = {
+        "own": x * 2 + zh, "own_z": x * 2 + 1 - zh,
+        "ahead": on_x * 2 + zh, "ahead_z": on_x * 2 + 1 - zh,
+        "behind": back_x * 2 + zh, "behind_z": back_x * 2 + 1 - zh,
+        "far": (x + 2) % 4 * 2 + zh, "far_z": (x + 2) % 4 * 2 + 1 - zh,
+    }
     sends = (
-        (own, zx), (own, xpd), (own, xmd), (own, sib),
-        (ownz, xpd), (ownz, xmd), (ownz, sib),
-        (source(xm, 0), xpd), (source(xp, 1), xmd),
-        (left, sib), (leftz, sib), (right, sib), (rightz, sib),
-        (far0, sib), (far1, sib),
+        ("own", on), ("own", back), ("own", zx), ("own", sib),
+        ("own_z", on), ("own_z", sib),
+        ("ahead", back), ("behind_z", on), ("ahead", zx),
+        ("behind", sib), ("ahead", sib), ("behind_z", sib),
+        ("far", sib), ("far_z", sib), ("ahead_z", sib),
     )
 
-    def send(w, *numbers):
+    def piece_copy(w, k):
+        slot = lbuf.at[w, q[sends[k][0]], core]
+        return remote(slot, slot, l_send.at[w, k], l_recv.at[w, q[sends[k][0]], core], sends[k][1])
+
+    def relay(w, arrived, numbers):
+        for name in arrived:
+            got(w, q[name], core)
         for k in numbers:
-            piece_copy(w, sends[k][0], sends[k][1], k).start()
+            piece_copy(w, k).start()
 
     def relay_a(w):
-        got(w, own, core)
-        send(w, 0, 1, 2, 3)
+        relay(w, ("own",), (0, 1, 2, 3))
 
     def relay_b(w):
-        got(w, ownz, core)
-        send(w, 4, 5, 6)
+        relay(w, ("own_z",), (4, 5))
 
     def relay_c(w):
-        for gs in (left, right, leftz, rightz):
-            got(w, gs, core)
-        send(w, 7, 8, 9, 10, 11, 12)
+        relay(w, ("ahead", "behind", "behind_z"), (6, 7, 8, 9, 10, 11))
 
     def relay_d(w):
-        got(w, far0, core)
-        got(w, far1, core)
-        send(w, 13, 14)
+        relay(w, ("far", "far_z", "ahead_z"), (12, 13, 14))
 
     def relay_e(w):
-        for gs in range(8):
-            got(w, gs, 1 - core)
+        for i in range(8):
+            got(w, i, 1 - core)
 
     def make_index():
         total = ktile[2] + krecv[3] + krecv[4] + krecv[5]
         rows = lax.broadcasted_iota(jnp.int32, (100, B), 0)
-        slots = [jnp.broadcast_to(pat[:, s : s + 1], (100, B)) for s in range(WL)]
-        for w in range(W):
-            kv = total[w : w + 1, :]
-            here = rows == kv
-            cols = ctile[w]
-            for o in range(1, 8):
-                cols = cols + crecv[(g + o) % 8, w]
-            idx = jnp.broadcast_to(kv * WL, (8, B))
+        owner = lax.broadcasted_iota(jnp.int32, (8, B), 1) // 16
+        crecv[g] = ctile[...]
+        rights = []
+        for s in range(1, WL):
+            slots = jnp.broadcast_to(pat[:, s : s + 1], (100, B))
+            parts = [
+                jnp.sum(jnp.where(rows == total[w : w + 1, :], slots, 0), axis=0, keepdims=True)
+                for w in range(W)
+            ]
+            rights.append(jnp.concatenate(parts + [jnp.zeros((8 - W, B), jnp.int32)], axis=0))
+        for m in range(WL):
+            cols = jnp.zeros((8, B), jnp.int32)
+            for t in range(8):
+                cols = jnp.where(owner == t, jnp.broadcast_to(crecv[t, :, m : m + 1], (8, B)), cols)
+            idx = total * WL
             for s in range(1, WL):
-                right = jnp.sum(jnp.where(here, slots[s], 0), axis=0, keepdims=True)
-                idx = idx + jnp.where(right == cols, s, 0)
-            idxv[w] = idx
+                idx = idx + jnp.where(rights[s - 1] == cols, s, 0)
+            idxv[m] = idx
         copy = pltpu.make_async_copy(idxv, idxs, i_sem)
         copy.start()
         copy.wait()
 
     def product(w, gs):
+        at = [place(gs, p) for p in range(2)]
         lc = jnp.concatenate(
-            [lbuf[w, gs, p, s] for p in range(2) for s in range(WL)], axis=1
+            [lbuf[w, at[p], p, s] for p in range(2) for s in range(WL)], axis=1
         )
 
         def block(m, l):
-            return rbuf[idxs[w, m, gs * 16 + l]]
+            return rbuf[idxs[m, w, gs * 16 + l]]
 
         rc = jnp.concatenate(
             [jnp.concatenate([block(m, l) for m in range(WL)], axis=1) for l in range(2 * WL)], axis=0
@@ -262,7 +277,7 @@
 
     def own_rows(w):
         def step(t):
-            acc[w % 2, t] = product(w, y * 2 + t)
+            acc[w % 3, t] = product(w, y * 2 + t)
 
         pair(step)
 
@@ -279,7 +294,7 @@
         a, b = 4 - 2 * tz, 3 + 2 * tz
         p_copy(w, b, zl_dev).wait_recv()
         p_copy(w, a, zl_dev).wait_recv()
-        return acc[w % 2, tz] + decode(precv.at[w, a]) + decode(precv.at[w, b])
+        return acc[w % 3, tz] + decode(precv.at[w, a]) + decode(precv.at[w, b])
 
     def cross(w):
         encode(psend.at[w, 6], plane_sum(w, 1 - zl))
@@ -299,8 +314,8 @@
                 c_s * s[:, m * B : (m + 1) * B] + c_o * o
             ).astype(BF16)
 
+    k_start()
     t_start(0)
-    k_start()
     t_start(1)
     for o in range(1, 8):
         c_copy(o).start()
@@ -312,28 +327,30 @@
     k_got(1)
     ktile[1] = krecv[0] + krecv[1]
     k_copy(ktile.at[1], 2, zx).start()
+    relay_a(1)
     relay_b(0)
-    t_start(3)
-    relay_a(1)
     k_got(2)
     ktile[2] = ktile[1] + krecv[2]
     k_copy(ktile.at[2], 3, xpd).start()
     k_copy(ktile.at[2], 4, xmd).start()
-    relay_b(1)
+    t_start(3)
     relay_c(0)
-    t_start(4)
     k_got(3)
     k_got(4)
     k_copy(krecv.at[3], 5, xpd).start()
+    relay_b(1)
+    t_start(4)
+    relay_a(2)
     for w in range(W):
         own_copy(w).start()
     for o in range(1, 8):
         remote(
             ctile, crecv.at[(g + o) % 8], c_send.at[o - 1], c_recv.at[(g + o) % 8], sib
         ).wait_recv()
+    k_got(5)
     relay_d(0)
-    k_got(5)
     make_index()
+    relay_b(2)
     r_copy.wait()
 
     def wave(w, carry):
@@ -347,34 +364,18 @@
             far_rows(v)
 
         guard(w < W, first, w)
-        guard(w < W - 2, relay_a, w + 2)
+        guard(w < W - 1, relay_c, w + 1)
         guard(w < W, near_rows, w)
-        guard(w < W - 1, relay_c, w + 1)
-        guard(w < W - 2, relay_b, w + 2)
         guard(w < W, own_rows, w)
+        guard(w < W - 3, relay_a, w + 3)
+        guard(w < W - 3, relay_b, w + 3)
+        guard(w < W - 1, relay_d, w + 1)
+        guard(jnp.logical_and(w > 0, w < W + 1), cross, w - 1)
         guard(w < W, joined_rows, w)
-        guard(w < W - 1, relay_d, w + 1)
+        guard(w > 1, finish, w - 2)
         return carry
 
-    def wave_tail(w, carry):
-        @pl.when(w > 0)
-        def _():
-            cross(w - 1)
-
-        wave_body(w)
-
-        @pl.when(w > 0)
-        def _():
-            finish(w - 1)
-
-        return carry
-
-    def wave_body(w):
-        @pl.when(w < W)
-        def _():
-            wave(w, 0)
-
-    lax.fori_loop(0, W + 1, wave_tail, 0)
+    lax.fori_loop(0, W + 2, wave, 0)
 
     def drain(w, carry):
         @pl.when(away)
@@ -382,7 +383,7 @@
             t_copy(w).wait_send()
 
         for k in range(15):
-            piece_copy(w, sends[k][0], sends[k][1], k).wait_send()
+            piece_copy(w, k).wait_send()
         for k in range(7):
             p_copy(w, k, zl_dev).wait_send()
         return carry
@@ -413,13 +414,13 @@
             pltpu.VMEM((W, 8, 2, WL, B, B), BF16),
             pltpu.VMEM((W, 7, PR, B), jnp.int16),
             pltpu.VMEM((W, 7, PR, B), jnp.int16),
-            pltpu.VMEM((W, 8, B), jnp.int32),
-            pltpu.VMEM((8, W, 8, B), jnp.int32),
+            pltpu.VMEM((8, B), jnp.int32),
+            pltpu.VMEM((8, 8, B), jnp.int32),
             pltpu.VMEM((3, 8, B), jnp.int32),
             pltpu.VMEM((6, 8, B), jnp.int32),
-            pltpu.VMEM((2, 2, B, R), F32),
-            pltpu.VMEM((W, 8, B), jnp.int32),
-            pltpu.SMEM((W, 8, B), jnp.int32),
+            pltpu.VMEM((3, 2, B, R), F32),
+            pltpu.VMEM((WL, 8, B), jnp.int32),
+            pltpu.SMEM((WL, 8, B), jnp.int32),
             dma((W,)), dma, dma((W,)), dma((W, 15)), dma((W, 8, 2)), dma((W, 7)), dma((W, 7)),
             dma((7,)), dma((8,)), dma((6,)), dma((6,)), dma,
         ],

time: 126 us -> 118 us (0.937)
  Pallas kernels: 120 us -> 113 us
    pallas_call x1, Pallas kernels: 120 us -> 113 us  [body(): pl.pallas_call(kernel, out_shape=jax.ShapeDtypeStruct((W, WL, B, B), BF16...]
where the time goes in v2:
time: 118 us; the launch traced here: 117 us
  Pallas kernels  113 us (96%)
  local copies, waits for them, and re-layouts  3.53 us (3%)
    pallas_call x1, Pallas kernels, body(): pl.pallas_call(kernel, out_shape=jax.ShapeDtypeStruct((W, WL, B, B), BF16...  113 us
    unnamed x2, local copies, waits for them, and re-layouts  3.53 us

profile of v2, /device:TPU:1, one launch (start us, length us, event | category | flops | bytes accessed | tf_op | source)
XLA Modules:
  0.0 116.8 jit_solution(1464242810755579318)
XLA Ops:
  0.0 1.4 %copy.4.pat = s32[100,5]{1,0:T(8,128)} copy(s32[100,5]{0,1:T(8,128)} %param.4) | data formatting | bytes 4000 | tf_op args[1]
  1.4 113.3 %shard_map.37 = bf16[5,5,128,128]{3,2,1,0:T(8,128)(2,1)} custom-call(s32[40]{0:T(128)} %flag_ref.1, bf16[500,128,128]{2,1,0:T(8,128)(2,1)} %bitcast.1, s32[100,5]{1,0:T(8,128)} %copy.4.pat), custom_call_target="tpu_custom_call" | custom-call | flops 8400000000 | bytes 20000000 | tf_op jit(solution)/shard_map/pallas_call | solution.py:406
  114.7 2.1 %copy.6 = bf16[5,5,128,128]{3,2,1,0:T(8,128)(2,1)} copy(bf16[5,5,128,128]{3,2,1,0:T(8,128)(2,1)} %shard_map.37) | data formatting | bytes 1638400

commit v3 on v2

--- a/solution.py
+++ b/solution.py
@@ -316,30 +316,31 @@
 
     k_start()
     t_start(0)
-    t_start(1)
     for o in range(1, 8):
         c_copy(o).start()
     r_copy.start()
     k_got(0)
     k_copy(krecv.at[0], 1, sib).start()
+    t_start(1)
     relay_a(0)
     t_start(2)
     k_got(1)
     ktile[1] = krecv[0] + krecv[1]
     k_copy(ktile.at[1], 2, zx).start()
-    relay_a(1)
     relay_b(0)
     k_got(2)
     ktile[2] = ktile[1] + krecv[2]
     k_copy(ktile.at[2], 3, xpd).start()
     k_copy(ktile.at[2], 4, xmd).start()
+    relay_a(1)
+    relay_c(0)
     t_start(3)
-    relay_c(0)
     k_got(3)
     k_got(4)
     k_copy(krecv.at[3], 5, xpd).start()
     relay_b(1)
     t_start(4)
+    relay_d(0)
     relay_a(2)
     for w in range(W):
         own_copy(w).start()
@@ -348,7 +349,6 @@
             ctile, crecv.at[(g + o) % 8], c_send.at[o - 1], c_recv.at[(g + o) % 8], sib
         ).wait_recv()
     k_got(5)
-    relay_d(0)
     make_index()
     relay_b(2)
     r_copy.wait()
@@ -365,8 +365,8 @@
 
         guard(w < W, first, w)
         guard(w < W - 1, relay_c, w + 1)
+        guard(w < W, own_rows, w)
         guard(w < W, near_rows, w)
-        guard(w < W, own_rows, w)
         guard(w < W - 3, relay_a, w + 3)
         guard(w < W - 3, relay_b, w + 3)
         guard(w < W - 1, relay_d, w + 1)

time: 118 us -> 117 us (level)
  no operation moved by 1% of the time
where the time goes in v3:
time: 117 us
  Pallas kernels  113 us (97%)
  local copies, waits for them, and re-layouts  3.53 us (3%)
    pallas_call x1, Pallas kernels, body(): pl.pallas_call(kernel, out_shape=jax.ShapeDtypeStruct((W, WL, B, B), BF16...  113 us
    unnamed x2, local copies, waits for them, and re-layouts  3.53 us

profile of v3, /device:TPU:1, one launch (start us, length us, event | category | flops | bytes accessed | tf_op | source)
XLA Modules:
  0.0 116.8 jit_solution(32069710987090794)
XLA Ops:
  0.0 1.4 %copy.4.pat = s32[100,5]{1,0:T(8,128)} copy(s32[100,5]{0,1:T(8,128)} %param.4) | data formatting | bytes 4000 | tf_op args[1]
  1.4 113.3 %shard_map.37 = bf16[5,5,128,128]{3,2,1,0:T(8,128)(2,1)} custom-call(s32[40]{0:T(128)} %flag_ref.1, bf16[500,128,128]{2,1,0:T(8,128)(2,1)} %bitcast.1, s32[100,5]{1,0:T(8,128)} %copy.4.pat), custom_call_target="tpu_custom_call" | custom-call | flops 8400000000 | bytes 20000000 | tf_op jit(solution)/shard_map/pallas_call | solution.py:406
  114.7 2.1 %copy.6 = bf16[5,5,128,128]{3,2,1,0:T(8,128)(2,1)} copy(bf16[5,5,128,128]{3,2,1,0:T(8,128)(2,1)} %shard_map.37) | data formatting | bytes 1638400
